TPU v7x, 256 devices: a whole 4x4x8 slice. The times are simulated.
256 devices in a mesh: lat: 8 (over y_hi, x), lon: 32 (over z, y_lo, core).
Axes of the slice: x: 4, y: 4 (y_hi: 2, y_lo: 2; y = y_hi * 2 + y_lo), z: 8, core: 2. Of those that a mesh axis runs over, the one named last changes fastest.
Arguments:
- queries: bfloat16 [128, 256, 768], P('lat', 'lon'), may hold values from -8 to 8
- key_vectors: bfloat16 [128, 256, 768], P('lat', 'lon'), may hold values from -8 to 8
- value_vectors: bfloat16 [128, 256, 768], P('lat', 'lon'), may hold values from -12 to 12
- upstream: bfloat16 [128, 256, 768], P('lat', 'lon'), may hold values from -6 to 6
- w_out: bfloat16 [768, 768], replicated, may hold values from -0.21875 to 0.21875
- neighbours: int32 [16, 32, 4], replicated, may hold values from 0 to 511, as said below
- counts: int32 [16, 32], replicated, may hold values from 2 to 4, as said below
Outputs:
- mixed_out: bfloat16 [128, 256, 768], P('lat', 'lon')
- q_grad: bfloat16 [128, 256, 768], P('lat', 'lon')
- k_grad: bfloat16 [128, 256, 768], P('lat', 'lon')
- v_grad: bfloat16 [128, 256, 768], P('lat', 'lon')
- w_grad: float32 [768, 768], replicated
Inputs may be any that keep to these rules, and one draw needn't show every extreme that they name: `neighbours`: entry s of block (i, j) names a block i2 * 32 + j2 with i2 within one of i and j2 within one of j around the longitude circle; slot 0 names the block itself, the entries of slots below counts[i, j] are distinct, and the slots at or beyond counts[i, j] name the block itself. `counts`: every block outside the first and the last row of blocks has 4.
All inputs are finite; a program needn't handle non-finite values.
Results may differ from a plain program's by a relative error of at most 0.03.
Values may be sent and summed in bfloat16 or wider, within the bound.
A program may use at most 64 MiB of HBM per device.

v0:
```python
import math
import jax
import jax.numpy as jnp
from jax import lax
from jax.sharding import PartitionSpec as P

HEADS = 12
HEAD_DIM = 64
BLK = 8
SLOTS = 4


def padded_2(value, sides, width, wrap):
    for axis, dim in sides:
        peers, length = (lax.axis_size(axis), value.shape[dim])
        up = [(i, (i + 1) % peers) for i in range(peers if wrap else peers - 1)]
        down = [(j, i) for i, j in up]
        last = lax.slice_in_dim(value, length - width, length, axis=dim)
        leading = lax.slice_in_dim(value, 0, width, axis=dim)
        before = lax.ppermute(last, axis, up)
        after = lax.ppermute(leading, axis, down)
        value = jnp.concatenate([before, value, after], axis=dim)
    return value


def to_blocks(token_grid):
    lat_rows, lon_cols, feat_width = token_grid.shape
    block_tiles = token_grid.reshape(
        lat_rows // BLK, BLK, lon_cols // BLK, BLK, feat_width
    ).transpose(0, 2, 1, 3, 4)
    return block_tiles.reshape(lat_rows // BLK * (lon_cols // BLK), BLK * BLK, feat_width)


def from_blocks(block_tiles, lat_blocks, lon_blocks):
    feat_width = block_tiles.shape[-1]
    token_grid = block_tiles.reshape(lat_blocks, lon_blocks, BLK, BLK, feat_width).transpose(
        0, 2, 1, 3, 4
    )
    return token_grid.reshape(lat_blocks * BLK, lon_blocks * BLK, feat_width)


def split_heads(block_tiles):
    return block_tiles.reshape(block_tiles.shape[0], block_tiles.shape[1], HEADS, HEAD_DIM)


def slot_places(
    neighbours,
    counts,
    first_lat,
    first_lon,
    grid_rows,
    grid_cols,
    anchor_lat,
    anchor_lon,
    pad_rows,
    pad_cols,
):
    total_lat = neighbours.shape[0]
    total_lon = neighbours.shape[1]
    block_lat = first_lat + jnp.arange(grid_rows, dtype=jnp.int32)
    block_lon = (first_lon + jnp.arange(grid_cols, dtype=jnp.int32)) % total_lon
    inside = (block_lat >= 0) & (block_lat < total_lat)
    safe_lat = jnp.clip(block_lat, 0, total_lat - 1)
    slot_table = jnp.take(jnp.take(neighbours, safe_lat, axis=0), block_lon, axis=1)
    slot_limit = jnp.take(jnp.take(counts, safe_lat, axis=0), block_lon, axis=1)
    slot_ids = jnp.arange(SLOTS, dtype=jnp.int32)
    rel_lat = slot_table // total_lon - anchor_lat
    rel_lon = (slot_table % total_lon - anchor_lon) % total_lon
    usable = (slot_ids[None, None, :] < slot_limit[:, :, None]) & inside[:, None, None]
    usable = usable & (rel_lat >= 0) & (rel_lat < pad_rows) & (rel_lon < pad_cols)
    key_place = jnp.where(usable, rel_lat * pad_cols + rel_lon, 0)
    return (
        key_place.reshape(grid_rows * grid_cols, SLOTS),
        usable.reshape(grid_rows * grid_cols, SLOTS),
    )


def gather_sets(padded_tiles, key_place):
    picked = jnp.take(padded_tiles, key_place.reshape(-1), axis=0)
    return picked.reshape(key_place.shape[0], SLOTS * BLK * BLK, padded_tiles.shape[-1])


def masked_scores(query_tiles, key_sets, key_valid):
    raw = jnp.einsum(
        "nqhd,nkhd->nhqk",
        split_heads(query_tiles),
        split_heads(key_sets),
        preferred_element_type=jnp.float32,
    )
    raw = raw * (1.0 / math.sqrt(HEAD_DIM))
    return jnp.where(key_valid[:, None, None, :], raw, -jnp.inf)


def forward_core(query_tiles, key_sets, value_sets, key_valid):
    masked = masked_scores(query_tiles, key_sets, key_valid)
    row_top = jnp.max(masked, axis=-1, keepdims=True)
    exp_total = jnp.sum(jnp.exp(masked - row_top), axis=-1, keepdims=True)
    log_total = row_top + jnp.log(exp_total)
    attn_probs = jnp.exp(masked - log_total)
    probs_low = attn_probs.astype(jnp.bfloat16)
    mixed_heads = jnp.einsum(
        "nhqk,nkhd->nqhd", probs_low, split_heads(value_sets), preferred_element_type=jnp.float32
    )
    attended = mixed_heads.astype(jnp.bfloat16).reshape(query_tiles.shape)
    return (attended, attn_probs, probs_low, log_total[..., 0])


def head_delta(d_att, attended):
    product = d_att.astype(jnp.float32) * attended.astype(jnp.float32)
    return jnp.sum(split_heads(product), axis=-1).transpose(0, 2, 1)


def backward_scores(attn_probs, d_att, row_delta, value_sets):
    dprobs = jnp.einsum(
        "nqhd,nkhd->nhqk",
        split_heads(d_att),
        split_heads(value_sets),
        preferred_element_type=jnp.float32,
    )
    return (attn_probs * (dprobs - row_delta[..., None]) * (1.0 / math.sqrt(HEAD_DIM))).astype(
        jnp.bfloat16
    )


def grad_queries(dscores, key_sets):
    summed = jnp.einsum(
        "nhqk,nkhd->nqhd", dscores, split_heads(key_sets), preferred_element_type=jnp.float32
    )
    return summed.astype(jnp.bfloat16).reshape(summed.shape[0], summed.shape[1], -1)


def contract_keys(weights_low, block_tiles):
    summed = jnp.einsum(
        "nhqk,nqhd->nkhd", weights_low, split_heads(block_tiles), preferred_element_type=jnp.float32
    )
    return summed.reshape(summed.shape[0], summed.shape[1], -1)


def add_into(contrib, key_place, usable, pad_count):
    flat_place = key_place.reshape(-1)
    feat_width = contrib.shape[-1]
    flat_terms = contrib.reshape(flat_place.shape[0], BLK * BLK * feat_width)
    flat_terms = jnp.where(usable.reshape(-1)[:, None], flat_terms, 0.0)
    summed = (
        jnp.zeros((pad_count, BLK * BLK * feat_width), jnp.float32).at[flat_place].add(flat_terms)
    )
    return summed.reshape(pad_count, BLK * BLK, feat_width)


def fold_lat(extended, lat_rows):
    interior = extended[:, 2 * BLK : 2 * BLK + lat_rows]
    interior = interior.at[:, :BLK].add(extended[:, :BLK])
    return interior.at[:, lat_rows - BLK :].add(extended[:, lat_rows + 3 * BLK :])


def fold_lon(extended, lon_cols):
    interior = extended[:, :, 2 * BLK : 2 * BLK + lon_cols]
    interior = interior.at[:, :, :BLK].add(extended[:, :, :BLK])
    return interior.at[:, :, lon_cols - BLK :].add(extended[:, :, lon_cols + 3 * BLK :])


def on_device(queries, key_vectors, value_vectors, upstream, w_out, neighbours, counts):
    lat_rows, lon_cols, feat_width = queries.shape
    lat_blocks = lat_rows // BLK
    lon_blocks = lon_cols // BLK
    pad_rows = lat_blocks + 2
    pad_cols = lon_blocks + 2
    pad_count = pad_rows * pad_cols
    inner_count = BLK * BLK
    tokens_all = lat_rows * lon_cols * lax.axis_size("lat") * lax.axis_size("lon")
    first_lat = lax.axis_index("lat") * lat_blocks
    first_lon = lax.axis_index("lon") * lon_blocks
    stacked = jnp.stack((key_vectors, value_vectors))
    lon_wide = padded_2(stacked, (("lon", 2),), BLK, True)
    padded = padded_2(lon_wide, (("lat", 1),), BLK, False)
    key_tiles = to_blocks(padded[0])
    value_tiles = to_blocks(padded[1])
    own_place, own_usable = slot_places(
        neighbours,
        counts,
        first_lat,
        first_lon,
        lat_blocks,
        lon_blocks,
        first_lat - 1,
        first_lon - 1,
        pad_rows,
        pad_cols,
    )
    query_tiles = to_blocks(queries)
    key_sets = gather_sets(key_tiles, own_place)
    value_sets = gather_sets(value_tiles, own_place)
    key_valid = jnp.repeat(own_usable, inner_count, axis=1)
    attended, attn_probs, probs_low, log_total = forward_core(
        query_tiles, key_sets, value_sets, key_valid
    )
    flat_att = attended.reshape(-1, feat_width)
    mixed_flat = jnp.dot(flat_att, w_out, preferred_element_type=jnp.float32).astype(jnp.bfloat16)
    grad_tiles = to_blocks(upstream)
    flat_grad = grad_tiles.reshape(-1, feat_width)
    local_weight = lax.dot_general(
        flat_att, flat_grad, (((0,), (0,)), ((), ())), preferred_element_type=jnp.float32
    )
    w_grad = lax.psum(local_weight, ("lat", "lon")) / math.sqrt(tokens_all)
    d_att = lax.dot_general(
        flat_grad, w_out, (((1,), (1,)), ((), ())), preferred_element_type=jnp.float32
    )
    d_att = d_att.astype(jnp.bfloat16).reshape(attended.shape)
    row_delta = head_delta(d_att, attended)
    dscores = backward_scores(attn_probs, d_att, row_delta, value_sets)
    query_grad = grad_queries(dscores, key_sets)
    key_contrib = contract_keys(dscores, query_tiles)
    value_contrib = contract_keys(probs_low, d_att)
    key_pad = from_blocks(
        add_into(key_contrib, own_place, own_usable, pad_count), pad_rows, pad_cols
    )
    value_pad = from_blocks(
        add_into(value_contrib, own_place, own_usable, pad_count), pad_rows, pad_cols
    )
    pad_terms = jnp.stack((key_pad, value_pad))
    extended = padded_2(pad_terms.astype(jnp.bfloat16), (("lat", 1),), BLK, False).astype(
        pad_terms.dtype
    )
    rows_done = fold_lat(extended, lat_rows)
    extended_lon = padded_2(rows_done.astype(jnp.bfloat16), (("lon", 2),), BLK, True).astype(
        rows_done.dtype
    )
    folded = fold_lon(extended_lon, lon_cols)
    key_grad = folded[0].astype(jnp.bfloat16)
    value_grad = folded[1].astype(jnp.bfloat16)
    mixed_out = from_blocks(mixed_flat.reshape(attended.shape), lat_blocks, lon_blocks)
    q_grad = from_blocks(query_grad, lat_blocks, lon_blocks)
    return (mixed_out, q_grad, key_grad, value_grad, w_grad)


def solution(mesh):
    return jax.shard_map(
        on_device,
        mesh=mesh,
        in_specs=(
            P("lat", "lon", None),
            P("lat", "lon", None),
            P("lat", "lon", None),
            P("lat", "lon", None),
            P(),
            P(),
            P(),
        ),
        out_specs=(
            P("lat", "lon", None),
            P("lat", "lon", None),
            P("lat", "lon", None),
            P("lat", "lon", None),
            P(),
        ),
        check_vma=False,
    )
```

profile of v0, /device:TPU:2, one launch (start us, length us, event | category | flops | bytes accessed | tf_op | source)
XLA Modules:
  0.0 395.0 jit_solution(1990365408183735528)
XLA Ops:
  8.4 6.4 %collective-permute-start.1 = (bf16[2,16,8,768]{3,2,1,0:T(8,128)(2,1)S(1)}, bf16[2,16,8,768]{3,2,1,0:T(8,128)(2,1)S(1)}, u32[]{:S(2)}, u32[]{:S(2)}) collective-permute-start(bf16[2,16,8,768]{3,2,1,0:T(8,128)(2,1)S(1)} %pad_maximum_fusion.6), channel_id=1, source_target_pairs={{1,0},{2,1},{3,2},{4,3},{5,4},{6,5},{7,6},{8,7},{9,8},{10,9},{11,1... | collective-permute-start | bytes 1179656 | tf_op jit(solution)/shard_map/ppermute | solution.py:21
  20.1 4.0 %collective-permute-done = bf16[2,16,8,768]{3,2,1,0:T(8,128)(2,1)S(1)} collective-permute-done((bf16[2,16,8,768]{3,2,1,0:T(8,128)(2,1)S(1)}, bf16[2,16,8,768]{3,2,1,0:T(8,128)(2,1)S(1)}, u32[]{:S(2)}, u32[]{:S(2)}) %collective-permute-start) | collective-permute-done | bytes 393248 | tf_op jit(solution)/shard_map/ppermute | solution.py:20
  25.3 2.4 collective-permute-start.3
  27.7 3.6 collective-permute-start.2
  35.3 2.5 collective-permute-done.3
  37.8 2.6 collective-permute-done.2
  45.2 2.5 broadcast_select_fusion.2
  47.7 2.7 reshape.642
  50.5 2.1 copy.37
  52.6 2.7 reshape.643
  55.4 2.1 copy.35
  65.3 4.7 %copy.46 = f32[2,256,12,64]{3,2,1,0:T(8,128)} copy(f32[2,256,12,64]{1,3,2,0:T(8,128)} %convolution_bitcast_fusion) | data formatting | bytes 3145728 | tf_op jit(solution)/shard_map/nhqk,nqhd->nkhd/transpose | solution.py:133
  70.1 4.4 %reshape_reshape.37 = f32[8,49152]{1,0:T(8,128)} reshape(f32[2,256,12,64]{3,2,1,0:T(8,128)} %copy.46) | data formatting | bytes 3145728 | tf_op jit(solution)/shard_map/reshape;reshape | solution.py:142
  74.5 3.7 copy.49
  78.2 4.5 %reshape_reshape.39 = f32[8,49152]{1,0:T(8,128)} reshape(f32[2,256,12,64]{3,2,1,0:T(8,128)} %copy.49) | data formatting | bytes 3145728 | tf_op jit(solution)/shard_map/reshape;reshape | solution.py:142
  82.7 3.4 broadcast_select_fusion.1
  86.1 5.1 %scatter_custom_fusion.1 = f32[12,49152]{1,0:T(8,128)} fusion(s32[8]{0:T(128)} %fusion.29, f32[8,49152]{1,0:T(8,128)} %get-tuple-element.106, f32[]{:T(128)} %constant.271.clone.1), kind=kCustom, calls=%fused_computation.14 | custom fusion | flops 393216 | bytes 2359808 | tf_op jit(solution)/shard_map/scatter-add | solution.py:145
  93.8 4.9 %scatter_custom_fusion = f32[12,49152]{1,0:T(8,128)} fusion(s32[8]{0:T(128)} %fusion.29, f32[8,49152]{1,0:T(8,128)} %get-tuple-element.105, f32[]{:T(128)} %constant.271.clone.1), kind=kCustom, calls=%fused_computation.16 | custom fusion | flops 393216 | bytes 2359808 | tf_op jit(solution)/shard_map/scatter-add | solution.py:145
  104.3 3.9 collective-permute-start.4
  111.3 2.9 fusion.17
  126.8 2.8 collective-permute-done.7
  129.6 5.1 %collective-permute-done.6 = bf16[2,16,8,768]{3,2,1,0:T(8,128)(2,1)} collective-permute-done((bf16[2,16,8,768]{3,2,1,0:T(8,128)(2,1)}, bf16[2,16,8,768]{3,2,1,0:T(8,128)(2,1)}, u32[]{:S(2)}, u32[]{:S(2)}) %collective-permute-start.6) | collective-permute-done | bytes 393248 | tf_op jit(solution)/shard_map/ppermute | solution.py:20
  136.8 248.1 %all-reduce.2.cloned.1.call-done = f32[768,768]{1,0:T(8,128)} async-done(((f32[768,768]{1,0:T(8,128)}), f32[768,768]{1,0:T(8,128)}) %all-reduce.2.cloned.1.call-update) | async-done | bytes 2359312 | tf_op jit(solution)/shard_map/psum | solution.py:204
  384.9 3.3 broadcast_multiply_fusion
  (101 shorter events, 49.9 us)
Async XLA Ops:
  7.2 11.0 %copy-start = (bf16[768,768]{1,0:T(8,128)(2,1)S(1)}, bf16[768,768]{1,0:T(8,128)(2,1)}, u32[]{:S(2)}) copy-start(bf16[768,768]{1,0:T(8,128)(2,1)} %param.25) | copy-start | bytes 3538948
  7.2 16.9 %copy-start.9 = (bf16[16,8,768]{2,1,0:T(8,128)(2,1)S(1)}, bf16[16,8,768]{2,1,0:T(8,128)(2,1)}, u32[]{:S(2)}) copy-start(bf16[16,8,768]{2,1,0:T(8,128)(2,1)} %param.23) | copy-start | bytes 589828
  7.2 16.9 %copy-start.10 = (bf16[16,8,768]{2,1,0:T(8,128)(2,1)S(1)}, bf16[16,8,768]{2,1,0:T(8,128)(2,1)}, u32[]{:S(2)}) copy-start(bf16[16,8,768]{2,1,0:T(8,128)(2,1)} %param.22) | copy-start | bytes 589828
  7.2 377.7 %all-reduce.2.cloned.1.call-start = ((), (), s32[]{:S(2)}) async-start(), calls=%async_computation | async-start | bytes 4718592 | tf_op jit(solution)/shard_map/psum | solution.py:204
  8.4 11.7 %collective-permute-start.1 = (bf16[2,16,8,768]{3,2,1,0:T(8,128)(2,1)S(1)}, bf16[2,16,8,768]{3,2,1,0:T(8,128)(2,1)S(1)}, u32[]{:S(2)}, u32[]{:S(2)}) collective-permute-start(bf16[2,16,8,768]{3,2,1,0:T(8,128)(2,1)S(1)} %pad_maximum_fusion.6), channel_id=1, source_target_pairs={{1,0},{2,1},{3,2},{4,3},{5,4},{6,5},{7,6},{8,7},{9,8},{10,9},{11,1... | collective-permute-start | bytes 1179656 | tf_op jit(solution)/shard_map/ppermute | solution.py:21
  14.8 9.3 %collective-permute-start = (bf16[2,16,8,768]{3,2,1,0:T(8,128)(2,1)S(1)}, bf16[2,16,8,768]{3,2,1,0:T(8,128)(2,1)S(1)}, u32[]{:S(2)}, u32[]{:S(2)}) collective-permute-start(bf16[2,16,8,768]{3,2,1,0:T(8,128)(2,1)S(1)} %pad_maximum_fusion.6), channel_id=1, source_target_pairs={{0,1},{1,2},{2,3},{3,4},{4,5},{5,6},{6,7},{7,8},{8,9},{9,10},{10,1... | collective-permute-start | bytes 1179656 | tf_op jit(solution)/shard_map/ppermute | solution.py:20
  24.2 8.9 %copy-start.13 = (bf16[16,8,768]{2,1,0:T(8,128)(2,1)S(1)}, bf16[16,8,768]{2,1,0:T(8,128)(2,1)}, u32[]{:S(2)}) copy-start(bf16[16,8,768]{2,1,0:T(8,128)(2,1)} %param.21) | copy-start | bytes 589828
  25.3 12.5 %collective-permute-start.3 = (bf16[2,8,24,768]{3,2,1,0:T(8,128)(2,1)}, bf16[2,8,24,768]{3,2,1,0:T(8,128)(2,1)}, u32[]{:S(2)}, u32[]{:S(2)}) collective-permute-start(bf16[2,8,24,768]{3,2,1,0:T(8,128)(2,1)} %get-tuple-element.102), channel_id=1, source_target_pairs={{32,0},{64,32},{96,64},{128,96},{160,128},{192,160},{224,192},{33,... | collective-permute-start | bytes 1769480 | tf_op jit(solution)/shard_map/ppermute | solution.py:21
  27.7 12.7 %collective-permute-start.2 = (bf16[2,8,24,768]{3,2,1,0:T(8,128)(2,1)}, bf16[2,8,24,768]{3,2,1,0:T(8,128)(2,1)}, u32[]{:S(2)}, u32[]{:S(2)}) collective-permute-start(bf16[2,8,24,768]{3,2,1,0:T(8,128)(2,1)} %get-tuple-element.101), channel_id=1, source_target_pairs={{0,32},{32,64},{64,96},{96,128},{128,160},{160,192},{192,224},{1,3... | collective-permute-start | bytes 1769480 | tf_op jit(solution)/shard_map/ppermute | solution.py:20
  43.7 1.5 copy-start.8
  57.5 2.4 copy-start.5
  59.9 1.1 copy-start.3
  62.2 1.6 copy-start.7
  62.9 0.9 copy-start.1
  78.2 4.6 %copy-start.6 = (f32[8,49152]{1,0:T(8,128)S(1)}, f32[8,49152]{1,0:T(8,128)}, u32[]{:S(2)}) copy-start(f32[8,49152]{1,0:T(8,128)} %reshape_reshape.37) | copy-start | bytes 4718596
  101.2 7.0 %copy-start.12 = (bf16[2,64,12,64]{1,3,2,0:T(8,128)(2,1)S(1)}, bf16[2,64,12,64]{1,3,2,0:T(8,128)(2,1)}, u32[]{:S(2)}) copy-start(bf16[2,64,12,64]{1,3,2,0:T(8,128)(2,1)} %get-tuple-element.114) | copy-start | bytes 589828
  102.4 12.1 %collective-permute-start.5 = (bf16[2,8,24,768]{3,2,1,0:T(8,128)(2,1)}, bf16[2,8,24,768]{3,2,1,0:T(8,128)(2,1)}, u32[]{:S(2)}, u32[]{:S(2)}) collective-permute-start(bf16[2,8,24,768]{3,2,1,0:T(8,128)(2,1)} %get-tuple-element.96), channel_id=1, source_target_pairs={{32,0},{64,32},{96,64},{128,96},{160,128},{192,160},{224,192},{33,... | collective-permute-start | bytes 1769480 | tf_op jit(solution)/shard_map/ppermute | solution.py:21
  104.3 12.1 %collective-permute-start.4 = (bf16[2,8,24,768]{3,2,1,0:T(8,128)(2,1)}, bf16[2,8,24,768]{3,2,1,0:T(8,128)(2,1)}, u32[]{:S(2)}, u32[]{:S(2)}) collective-permute-start(bf16[2,8,24,768]{3,2,1,0:T(8,128)(2,1)} %get-tuple-element.95), channel_id=1, source_target_pairs={{0,32},{32,64},{64,96},{96,128},{128,160},{160,192},{192,224},{1,3... | collective-permute-start | bytes 1769480 | tf_op jit(solution)/shard_map/ppermute | solution.py:20
  121.0 3.0 copy-start.2
  121.0 3.0 copy-start.4
  121.9 7.7 %collective-permute-start.7 = (bf16[2,16,8,768]{3,2,1,0:T(8,128)(2,1)}, bf16[2,16,8,768]{3,2,1,0:T(8,128)(2,1)}, u32[]{:S(2)}, u32[]{:S(2)}) collective-permute-start(bf16[2,16,8,768]{3,2,1,0:T(8,128)(2,1)} %get-tuple-element.100), channel_id=1, source_target_pairs={{1,0},{2,1},{3,2},{4,3},{5,4},{6,5},{7,6},{8,7},{9,8},{10,9},{11,1... | collective-permute-start | bytes 1179656 | tf_op jit(solution)/shard_map/ppermute | solution.py:21
  124.0 1.8 copy-start.11
  124.0 10.7 %collective-permute-start.6 = (bf16[2,16,8,768]{3,2,1,0:T(8,128)(2,1)}, bf16[2,16,8,768]{3,2,1,0:T(8,128)(2,1)}, u32[]{:S(2)}, u32[]{:S(2)}) collective-permute-start(bf16[2,16,8,768]{3,2,1,0:T(8,128)(2,1)} %get-tuple-element.99), channel_id=1, source_target_pairs={{0,1},{1,2},{2,3},{3,4},{4,5},{5,6},{6,7},{7,8},{8,9},{9,10},{10,1... | collective-permute-start | bytes 1179656 | tf_op jit(solution)/shard_map/ppermute | solution.py:20
Sparse Core Ops, SparseCore 0:
  114.3 270.4 all-reduce.1
where the time goes:
time: 396 us; the launch traced here: 395 us
  waiting for transfers between devices  268 us (68%)
  local copies, waits for them, and re-layouts  46.5 us (12%)
  other arithmetic  34.4 us (9%)
  starting transfers between devices  20.4 us (5%)
  between operations  14.4 us (4%)
  matrix products  11.4 us (3%)
    psum x1, waiting for transfers between devices, on_device(): w_grad = lax.psum(local_weight, ('lat', 'lon')) / math.sqrt(tokens_all)  248 us
    ppermute x4, waiting for transfers between devices, padded_2(): before = lax.ppermute(last, axis, up)  13.7 us
    ppermute x4, starting transfers between devices, padded_2(): after = lax.ppermute(leading, axis, down)  12.8 us
    another operation x8, local copies, waits for them, and re-layouts, split_heads(): block_tiles.reshape(block_tiles.shape[0], block_tiles.shape[1], HEADS, HE...  12.7 us
    scatter-add x2, other arithmetic, add_into(): jnp.zeros((pad_count, BLK * BLK * feat_width), jnp.float32).at[flat_place]  10 us
    another operation x2, local copies, waits for them, and re-layouts, add_into(): flat_terms = contrib.reshape(flat_place.shape[0], BLK * BLK * feat_width)  8.94 us
    transpose x2, local copies, waits for them, and re-layouts, contract_keys(): jnp.einsum('nhqk,nqhd->nkhd', weights_low, split_heads(block_tiles), pref...  8.45 us
  transfers between devices with their start and end apart: 9, of which 9 were waited for; matrix products, arithmetic and copies ran while one was open for 6% of the time, Pallas kernels for 0%

commit v1 on v0

--- a/solution.py
+++ b/solution.py
@@ -201,7 +201,7 @@
     local_weight = lax.dot_general(
         flat_att, flat_grad, (((0,), (0,)), ((), ())), preferred_element_type=jnp.float32
     )
-    w_grad = lax.psum(local_weight, ("lat", "lon")) / math.sqrt(tokens_all)
+    w_grad = lax.psum(lax.psum(local_weight, "lat"), "lon") / math.sqrt(tokens_all)
     d_att = lax.dot_general(
         flat_grad, w_out, (((1,), (1,)), ((), ())), preferred_element_type=jnp.float32
     )

time: 396 us -> 443 us (1.12)
  waiting for transfers between devices: 268 us -> 316 us
    psum x1 -> x2, waiting for transfers between devices: 248 us -> 300 us  [the longest x1 218 us: on_device(): lax.psum(lax.psum(local_weight, 'lat'), 'lon') / math.sqrt(tokens_all)]
  transfers between devices with their start and end apart: 9 -> 10, of which waited for: 9 -> 8; matrix products, arithmetic and copies ran while one was open for 6% -> 9% of each run, Pallas kernels for 0% -> 0%
where the time goes in v1:
time: 443 us; the launch traced here: 442 us
  waiting for transfers between devices  316 us (71%)
  local copies, waits for them, and re-layouts  46.6 us (11%)
  other arithmetic  35 us (8%)
  starting transfers between devices  18.6 us (4%)
  between operations  14.4 us (3%)
  matrix products  11.3 us (3%)
    psum x1, waiting for transfers between devices, on_device(): lax.psum(lax.psum(local_weight, 'lat'), 'lon') / math.sqrt(tokens_all)  218 us
    psum x1, waiting for transfers between devices, on_device(): lax.psum(local_weight, 'lat')  81.8 us
    another operation x8, local copies, waits for them, and re-layouts, split_heads(): block_tiles.reshape(block_tiles.shape[0], block_tiles.shape[1], HEADS, HE...  12.7 us
    ppermute x4, starting transfers between devices, padded_2(): after = lax.ppermute(leading, axis, down)  10.7 us
    ppermute x4, waiting for transfers between devices, padded_2(): before = lax.ppermute(last, axis, up)  10.7 us
    scatter-add x2, other arithmetic, add_into(): jnp.zeros((pad_count, BLK * BLK * feat_width), jnp.float32).at[flat_place]  10.1 us
    another operation x2, local copies, waits for them, and re-layouts, add_into(): flat_terms = contrib.reshape(flat_place.shape[0], BLK * BLK * feat_width)  9.09 us
  transfers between devices with their start and end apart: 10, of which 8 were waited for; matrix products, arithmetic and copies ran while one was open for 9% of the time, Pallas kernels for 0%

profile of v1, /device:TPU:2, one launch (start us, length us, event | category | flops | bytes accessed | tf_op | source)
XLA Modules:
  0.0 441.6 jit_solution(17331855381126839834)
XLA Ops:
  8.4 6.4 %collective-permute-start.1 = (bf16[2,16,8,768]{3,2,1,0:T(8,128)(2,1)S(1)}, bf16[2,16,8,768]{3,2,1,0:T(8,128)(2,1)S(1)}, u32[]{:S(2)}, u32[]{:S(2)}) collective-permute-start(bf16[2,16,8,768]{3,2,1,0:T(8,128)(2,1)S(1)} %pad_maximum_fusion.6), channel_id=1, source_target_pairs={{1,0},{2,1},{3,2},{4,3},{5,4},{6,5},{7,6},{8,7},{9,8},{10,9},{11,1... | collective-permute-start | bytes 1179656 | tf_op jit(solution)/shard_map/ppermute | solution.py:21
  20.1 4.0 collective-permute-done
  25.3 2.4 collective-permute-start.3
  27.7 3.4 collective-permute-start.2
  35.6 2.2 collective-permute-done.3
  37.8 2.6 collective-permute-done.2
  45.2 2.5 broadcast_select_fusion.2
  47.7 2.7 reshape.642
  50.5 2.1 copy.37
  52.6 2.7 reshape.643
  55.4 2.2 copy.35
  68.7 3.7 copy.46
  72.4 4.6 %reshape_reshape.37 = f32[8,49152]{1,0:T(8,128)} reshape(f32[2,256,12,64]{3,2,1,0:T(8,128)} %copy.46) | data formatting | bytes 3145728 | tf_op jit(solution)/shard_map/reshape;reshape | solution.py:142
  77.0 3.7 copy.49
  80.7 4.5 %reshape_reshape.39 = f32[8,49152]{1,0:T(8,128)} reshape(f32[2,256,12,64]{3,2,1,0:T(8,128)} %copy.49) | data formatting | bytes 3145728 | tf_op jit(solution)/shard_map/reshape;reshape | solution.py:142
  88.6 3.4 broadcast_select_fusion.1
  91.9 5.1 %scatter_custom_fusion.1 = f32[12,49152]{1,0:T(8,128)} fusion(s32[8]{0:T(128)} %fusion.29, f32[8,49152]{1,0:T(8,128)} %get-tuple-element.106, f32[]{:T(128)} %constant.271.clone.1), kind=kCustom, calls=%fused_computation.14 | custom fusion | flops 393216 | bytes 2359808 | tf_op jit(solution)/shard_map/scatter-add | solution.py:145
  99.6 4.9 %scatter_custom_fusion = f32[12,49152]{1,0:T(8,128)} fusion(s32[8]{0:T(128)} %fusion.29, f32[8,49152]{1,0:T(8,128)} %get-tuple-element.105, f32[]{:T(128)} %constant.271.clone.1), kind=kCustom, calls=%fused_computation.16 | custom fusion | flops 393216 | bytes 2359808 | tf_op jit(solution)/shard_map/scatter-add | solution.py:145
  110.2 3.9 collective-permute-start.4
  114.2 81.8 %all-reduce.3.cloned.1.call-done = f32[768,768]{1,0:T(8,128)} async-done(((f32[768,768]{1,0:T(8,128)}), f32[768,768]{1,0:T(8,128)}) %all-reduce.3.cloned.1.call-update) | async-done | bytes 2359312 | tf_op jit(solution)/shard_map/psum | solution.py:204
  205.0 2.1 collective-permute-done.7
  207.1 4.1 collective-permute-done.6
  213.3 218.2 %all-reduce.5.cloned.1.call-done = f32[768,768]{1,0:T(8,128)} async-done(((f32[768,768]{1,0:T(8,128)}), f32[768,768]{1,0:T(8,128)}) %all-reduce.5.cloned.1.call-update) | async-done | bytes 2359312 | tf_op jit(solution)/shard_map/psum | solution.py:204
  431.4 3.3 broadcast_multiply_fusion
  (110 shorter events, 50.4 us)
Async XLA Ops:
  7.2 11.0 %copy-start = (bf16[768,768]{1,0:T(8,128)(2,1)S(1)}, bf16[768,768]{1,0:T(8,128)(2,1)}, u32[]{:S(2)}) copy-start(bf16[768,768]{1,0:T(8,128)(2,1)} %param.25) | copy-start | bytes 3538948
  7.2 16.9 %copy-start.10 = (bf16[16,8,768]{2,1,0:T(8,128)(2,1)S(1)}, bf16[16,8,768]{2,1,0:T(8,128)(2,1)}, u32[]{:S(2)}) copy-start(bf16[16,8,768]{2,1,0:T(8,128)(2,1)} %param.23) | copy-start | bytes 589828
  7.2 16.9 %copy-start.11 = (bf16[16,8,768]{2,1,0:T(8,128)(2,1)S(1)}, bf16[16,8,768]{2,1,0:T(8,128)(2,1)}, u32[]{:S(2)}) copy-start(bf16[16,8,768]{2,1,0:T(8,128)(2,1)} %param.22) | copy-start | bytes 589828
  7.2 188.7 %all-reduce.3.cloned.1.call-start = ((), (), s32[]{:S(2)}) async-start(), calls=%async_computation | async-start | bytes 4718592 | tf_op jit(solution)/shard_map/psum | solution.py:204
  8.4 11.7 %collective-permute-start.1 = (bf16[2,16,8,768]{3,2,1,0:T(8,128)(2,1)S(1)}, bf16[2,16,8,768]{3,2,1,0:T(8,128)(2,1)S(1)}, u32[]{:S(2)}, u32[]{:S(2)}) collective-permute-start(bf16[2,16,8,768]{3,2,1,0:T(8,128)(2,1)S(1)} %pad_maximum_fusion.6), channel_id=1, source_target_pairs={{1,0},{2,1},{3,2},{4,3},{5,4},{6,5},{7,6},{8,7},{9,8},{10,9},{11,1... | collective-permute-start | bytes 1179656 | tf_op jit(solution)/shard_map/ppermute | solution.py:21
  14.8 9.3 %collective-permute-start = (bf16[2,16,8,768]{3,2,1,0:T(8,128)(2,1)S(1)}, bf16[2,16,8,768]{3,2,1,0:T(8,128)(2,1)S(1)}, u32[]{:S(2)}, u32[]{:S(2)}) collective-permute-start(bf16[2,16,8,768]{3,2,1,0:T(8,128)(2,1)S(1)} %pad_maximum_fusion.6), channel_id=1, source_target_pairs={{0,1},{1,2},{2,3},{3,4},{4,5},{5,6},{6,7},{7,8},{8,9},{9,10},{10,1... | collective-permute-start | bytes 1179656 | tf_op jit(solution)/shard_map/ppermute | solution.py:20
  24.2 8.7 %copy-start.15 = (bf16[16,8,768]{2,1,0:T(8,128)(2,1)S(1)}, bf16[16,8,768]{2,1,0:T(8,128)(2,1)}, u32[]{:S(2)}) copy-start(bf16[16,8,768]{2,1,0:T(8,128)(2,1)} %param.21) | copy-start | bytes 589828
  25.3 12.5 %collective-permute-start.3 = (bf16[2,8,24,768]{3,2,1,0:T(8,128)(2,1)}, bf16[2,8,24,768]{3,2,1,0:T(8,128)(2,1)}, u32[]{:S(2)}, u32[]{:S(2)}) collective-permute-start(bf16[2,8,24,768]{3,2,1,0:T(8,128)(2,1)} %get-tuple-element.102), channel_id=1, source_target_pairs={{32,0},{64,32},{96,64},{128,96},{160,128},{192,160},{224,192},{33,... | collective-permute-start | bytes 1769480 | tf_op jit(solution)/shard_map/ppermute | solution.py:21
  27.7 12.7 %collective-permute-start.2 = (bf16[2,8,24,768]{3,2,1,0:T(8,128)(2,1)}, bf16[2,8,24,768]{3,2,1,0:T(8,128)(2,1)}, u32[]{:S(2)}, u32[]{:S(2)}) collective-permute-start(bf16[2,8,24,768]{3,2,1,0:T(8,128)(2,1)} %get-tuple-element.101), channel_id=1, source_target_pairs={{0,32},{32,64},{64,96},{96,128},{128,160},{160,192},{192,224},{1,3... | collective-permute-start | bytes 1769480 | tf_op jit(solution)/shard_map/ppermute | solution.py:20
  43.7 1.5 copy-start.9
  57.5 2.4 copy-start.5
  59.9 1.6 copy-start.3
  65.7 2.6 copy-start.8
  72.4 4.6 %copy-start.6 = (f32[2,256,12,64]{1,3,2,0:T(8,128)S(1)}, f32[2,256,12,64]{1,3,2,0:T(8,128)}, u32[]{:S(2)}) copy-start(f32[2,256,12,64]{1,3,2,0:T(8,128)} %convolution_bitcast_fusion.1) | copy-start | bytes 4718596
  80.7 4.5 %copy-start.12 = (bf16[128,768]{0,1:T(8,128)(2,1)S(1)}, bf16[128,768]{0,1:T(8,128)(2,1)}, u32[]{:S(2)}) copy-start(bf16[128,768]{0,1:T(8,128)(2,1)} %reshape_reshape.35) | copy-start | bytes 589828
  80.7 4.5 %copy-start.14 = (bf16[16,8,768]{2,1,0:T(8,128)(2,1)S(1)}, bf16[16,8,768]{2,1,0:T(8,128)(2,1)}, u32[]{:S(2)}) copy-start(bf16[16,8,768]{2,1,0:T(8,128)(2,1)} %param.24) | copy-start | bytes 589828
  87.2 344.3 %all-reduce.5.cloned.1.call-start = ((), (), s32[]{:S(2)}) async-start(), calls=%async_computation.1 | async-start | bytes 4718592 | tf_op jit(solution)/shard_map/psum | solution.py:204
  108.3 87.6 %collective-permute-start.5 = (bf16[2,8,24,768]{3,2,1,0:T(8,128)(2,1)}, bf16[2,8,24,768]{3,2,1,0:T(8,128)(2,1)}, u32[]{:S(2)}, u32[]{:S(2)}) collective-permute-start(bf16[2,8,24,768]{3,2,1,0:T(8,128)(2,1)} %get-tuple-element.96), channel_id=1, source_target_pairs={{32,0},{64,32},{96,64},{128,96},{160,128},{192,160},{224,192},{33,... | collective-permute-start | bytes 1769480 | tf_op jit(solution)/shard_map/ppermute | solution.py:21
  110.2 85.7 %collective-permute-start.4 = (bf16[2,8,24,768]{3,2,1,0:T(8,128)(2,1)}, bf16[2,8,24,768]{3,2,1,0:T(8,128)(2,1)}, u32[]{:S(2)}, u32[]{:S(2)}) collective-permute-start(bf16[2,8,24,768]{3,2,1,0:T(8,128)(2,1)} %get-tuple-element.95), channel_id=1, source_target_pairs={{0,32},{32,64},{64,96},{96,128},{128,160},{160,192},{192,224},{1,3... | collective-permute-start | bytes 1769480 | tf_op jit(solution)/shard_map/ppermute | solution.py:20
  200.5 1.5 copy-start.2
  200.5 1.6 copy-start.4
  201.5 5.7 %collective-permute-start.7 = (bf16[2,16,8,768]{3,2,1,0:T(8,128)(2,1)}, bf16[2,16,8,768]{3,2,1,0:T(8,128)(2,1)}, u32[]{:S(2)}, u32[]{:S(2)}) collective-permute-start(bf16[2,16,8,768]{3,2,1,0:T(8,128)(2,1)} %get-tuple-element.100), channel_id=1, source_target_pairs={{1,0},{2,1},{3,2},{4,3},{5,4},{6,5},{7,6},{8,7},{9,8},{10,9},{11,1... | collective-permute-start | bytes 1179656 | tf_op jit(solution)/shard_map/ppermute | solution.py:21
  201.5 2.5 copy-start.13
  201.5 9.7 %collective-permute-start.6 = (bf16[2,16,8,768]{3,2,1,0:T(8,128)(2,1)}, bf16[2,16,8,768]{3,2,1,0:T(8,128)(2,1)}, u32[]{:S(2)}, u32[]{:S(2)}) collective-permute-start(bf16[2,16,8,768]{3,2,1,0:T(8,128)(2,1)} %get-tuple-element.99), channel_id=1, source_target_pairs={{0,1},{1,2},{2,3},{3,4},{4,5},{5,6},{6,7},{7,8},{8,9},{9,10},{10,1... | collective-permute-start | bytes 1179656 | tf_op jit(solution)/shard_map/ppermute | solution.py:20
  (3 other events, 3.7 us)
Sparse Core Ops, SparseCore 0:
  87.3 108.5 all-reduce.2
  198.6 232.8 all-reduce.4
